TPU v7x, 128 devices: a whole 4x4x4 slice. The times are simulated.
128 devices in a mesh: fsdp: 4 (over z_hi, core), vocab: 32 (over y, x, z_lo).
Axes of the slice: x: 4, y: 4, z: 4 (z_hi: 2, z_lo: 2; z = z_hi * 2 + z_lo), core: 2. Of those that a mesh axis runs over, the one named last changes fastest.
Arguments:
- head_table: bfloat16 [81920, 7168], P('vocab', 'fsdp'), may hold values from -32 to 32
- embed_table: bfloat16 [81920, 7168], P('vocab', 'fsdp'), may hold values from -6 to 6
- hidden: bfloat16 [4, 256, 7168], P(None, ('fsdp', 'vocab')), may hold values from -128 to 128
- norm_gain: float32 [7168], replicated, may hold values from 0.5 to 1.5
- tokens: int32 [4, 256], P(None, 'fsdp'), may hold values from 0 to 81919
Outputs:
- logprobs: float32 [4, 256], P(None, 'fsdp')
- embeddings: bfloat16 [4, 256, 7168], P(None, 'vocab', 'fsdp')
All inputs are finite; a program needn't handle non-finite values.
Results may differ from a plain program's by a relative error of at most 0.0055.
Values may be sent and summed in bfloat16 or wider, within the bound.
A program may use at most 256 MiB of HBM per device.

v0:
```python
import jax
import jax.numpy as jnp
from jax import lax
from jax.sharding import PartitionSpec as P

QB = 128


def dequantize_group(group):
    rows_in, width = group.shape
    blocks = group.astype(jnp.float32).reshape(rows_in, width // QB, QB)
    largest = jnp.max(jnp.abs(blocks), axis=(0, 2), keepdims=True)
    scales = (largest + 1e-06) / 7.0
    coded = jnp.floor(blocks / scales + 0.5)
    return (coded * scales).astype(jnp.bfloat16).reshape(rows_in, width)


def dequantize(weights):
    height, width = weights.shape
    groups = weights.reshape(height // QB, QB, width)
    return lax.map(dequantize_group, groups).reshape(height, width)


def normalize(hidden, norm_gain):
    values = hidden.astype(jnp.float32)
    mean_square = jnp.mean(values * values, axis=-1, keepdims=True)
    return (values * lax.rsqrt(mean_square + 1e-06) * norm_gain).astype(jnp.bfloat16)


def block_logits(normed_rows, head_rows):
    return lax.dot_general(
        normed_rows, head_rows, (((1,), (1,)), ((), ())), preferred_element_type=jnp.float32
    )


def on_device(head_table, embed_table, hidden, norm_gain, tokens):
    owned_rows = head_table.shape[0]
    normed_local = normalize(hidden, norm_gain)
    normed_all = lax.all_gather(normed_local, "vocab", axis=1, tiled=True)
    step_count, row_count, width = normed_all.shape
    normed = normed_all.reshape(step_count * row_count, width)
    head_rows = lax.all_gather(head_table, "fsdp", axis=1, tiled=True)
    restored = dequantize(head_rows)
    logits = block_logits(normed, restored)
    local_tokens = tokens.reshape(step_count * row_count) - lax.axis_index("vocab") * owned_rows
    matches = lax.broadcasted_iota(jnp.int32, (1, owned_rows), 1) == local_tokens[:, None]
    targets = jnp.sum(jnp.where(matches, logits, 0.0), axis=1)
    maxima = jnp.max(logits, axis=1)
    maxima = lax.pmax(maxima, "vocab")
    totals = jnp.sum(jnp.exp(logits - maxima[:, None]), axis=1)
    totals, targets = lax.psum((totals, targets), "vocab")
    logprobs = (targets - maxima - jnp.log(totals)).reshape(step_count, row_count)
    every_token = lax.all_gather(tokens, "fsdp", axis=1, tiled=True)
    stored = embed_table.shape[0]
    local_entries = every_token - lax.axis_index("vocab") * stored
    inside = (local_entries >= 0) & (local_entries < stored)
    picked = jnp.take(embed_table, jnp.clip(local_entries, 0, stored - 1), axis=0).astype(
        jnp.float32
    )
    picked = jnp.where(inside[..., None], picked, 0.0)
    embeddings = lax.psum_scatter(
        picked.astype(jnp.bfloat16), "vocab", scatter_dimension=1, tiled=True
    )
    return (logprobs, embeddings)


def solution(mesh):
    placed = (
        P("vocab", "fsdp"),
        P("vocab", "fsdp"),
        P(None, ("fsdp", "vocab"), None),
        P(),
        P(None, "fsdp"),
    )
    return jax.shard_map(
        on_device,
        mesh=mesh,
        in_specs=placed,
        out_specs=(P(None, "fsdp"), P(None, "vocab", "fsdp")),
        check_vma=False,
    )
```

profile of v0, /device:TPU:0, one launch (start us, length us, event | category | flops | bytes accessed | tf_op | source)
XLA Modules:
  0.0 856.8 jit_solution(15240096991687232308)
XLA Ops:
  10.1 7.3 all-gather
  17.6 12.7 %gather_fusion = bf16[1024,1792]{1,0:T(8,128)(2,1)} fusion(bf16[2560,1792]{1,0:T(8,128)(2,1)} %param.8, s32[1024]{0:T(1024)S(1)} %broadcast_clamp_fusion), kind=kCustom, calls=%fused_computation | custom fusion | bytes 7344128 | tf_op jit(solution)/shard_map/jit(_take)/gather | solution.py:57
  39.1 130.7 %all-gather.4.cloned.1.call-done = bf16[4,64,7168]{2,0,1:T(4,128)(2,1)} async-done(((bf16[4,2,7168]{2,0,1:T(4,128)(2,1)}), bf16[4,64,7168]{2,0,1:T(4,128)(2,1)}) %all-gather.4.cloned.1.call-update) | async-done | bytes 3670032 | tf_op jit(solution)/shard_map/all_gather | solution.py:39
  169.8 5.0 copy.17
  174.8 165.3 %reduce-scatter.4.cloned.1.call-done = bf16[8,7168]{1,0:T(8,128)(2,1)} async-done(((bf16[256,7168]{1,0:T(8,128)(2,1)}), bf16[8,7168]{1,0:T(8,128)(2,1)}) %reduce-scatter.4.cloned.1.call-update) | async-done | bytes 114704
  341.8 222.1 %all-gather.6.cloned.1.call-done = bf16[2560,7168]{1,0:T(8,128)(2,1)} async-done(((bf16[2560,1792]{1,0:T(8,128)(2,1)}), bf16[2560,7168]{1,0:T(8,128)(2,1)}) %all-gather.6.cloned.1.call-update) | async-done | bytes 36700176 | tf_op jit(solution)/shard_map/all_gather | solution.py:42
  563.8 108.4 %while.10 = (s32[]{:T(128)}, bf16[20,128,7168]{2,1,0:T(8,128)(2,1)}, bf16[20,128,7168]{2,1,0:T(8,128)(2,1)}, s32[]{:T(128)}) while((s32[]{:T(128)}, bf16[20,128,7168]{2,1,0:T(8,128)(2,1)}, bf16[20,128,7168]{2,1,0:T(8,128)(2,1)}, s32[]{:T(128)}) %tuple.33), condition=%wide.region_4.5_spmd, body=%wide.region_1.4_spmd.sunk | while | flops 8257594 | bytes 5621177 | solution.py:21
  565.8 3.5 fusion.16
  576.6 3.5 fusion.16
  582.0 3.5 fusion.16
  592.9 3.5 fusion.16
  603.7 3.5 fusion.16
  609.1 3.5 fusion.16
  614.5 3.5 fusion.16
  620.0 3.5 fusion.16
  630.8 3.5 fusion.16
  641.5 3.5 fusion.16
  652.4 3.5 fusion.16
  657.8 3.5 fusion.16
  663.3 3.5 fusion.16
  668.7 3.5 fusion.16
  672.2 17.7 %fusion.10 = (f32[256]{0:T(256)S(1)}, f32[256,2560]{1,0:T(8,128)S(1)}) fusion(bf16[256,7168]{1,0:T(8,128)(2,1)} %bitcast.39, bf16[2560,7168]{1,0:T(8,128)(2,1)} %bitcast.44), kind=kOutput, calls=%fused_computation.30 | convolution fusion | flops 9395896320 | bytes 42992640 | tf_op jit(solution)/shard_map/dot_general | solution.py:31
  690.0 81.8 %pmax.7 = f32[256]{0:T(256)S(1)} all-reduce(f32[256]{0:T(256)S(1)} %get-tuple-element.30), channel_id=1, replica_groups=mesh['fsdp'=4,'vocab'=32] {'vocab'}, use_global_device_ids=true, to_apply=%region_8.9 | all-reduce | flops 256 | bytes 2048 | tf_op jit(solution)/shard_map/pmax | solution.py:49
  772.7 76.9 %all-reduce = (f32[256]{0:T(256)S(1)}, f32[256]{0:T(256)S(1)}) all-reduce(f32[256]{0:T(256)S(1)} %get-tuple-element.21, f32[256]{0:T(256)S(1)} %get-tuple-element.20), channel_id=1, replica_groups=mesh['fsdp'=4,'vocab'=32] {'vocab'}, use_global_device_ids=true, to_apply=%region_10.11 | all-reduce | flops 512 | bytes 4096 | tf_op jit(solution)/shard_map/psum | solution.py:51
  (118 shorter events, 74.3 us)
Async XLA Ops:
  7.2 162.7 %all-gather.4.cloned.1.call-start = ((), (), s32[]{:S(2)}) async-start(), calls=%async_computation.1 | async-start | bytes 3784704 | tf_op jit(solution)/shard_map/all_gather | solution.py:39
  10.0 330.1 %reduce-scatter.4.cloned.1.call-start = ((), (), s32[]{:S(2)}) async-start(), calls=%async_computation.3 | async-start | bytes 3784704
  38.3 0.8 copy-start
  38.3 525.6 %all-gather.6.cloned.1.call-start = ((), (), s32[]{:S(2)}) async-start(), calls=%async_computation.2 | async-start | bytes 45875200 | tf_op jit(solution)/shard_map/all_gather | solution.py:42
Sparse Core Ops, SparseCore 0:
  10.2 159.5 all-gather.3
  172.2 167.8 reduce-scatter.3
  341.9 221.8 all-gather.5
where the time goes:
time: 858 us; the launch traced here: 857 us
  waiting for transfers between devices  519 us (60%)
  blocking collectives  166 us (19%)
  other arithmetic  113 us (13%)
  local copies, waits for them, and re-layouts  27 us (3%)
  matrix products  17.7 us (2%)
  between operations  13.8 us (2%)
    all_gather x1, waiting for transfers between devices, on_device(): head_rows = lax.all_gather(head_table, 'fsdp', axis=1, tiled=True)  222 us
    unnamed x4, waiting for transfers between devices  166 us
    all_gather x1, waiting for transfers between devices, on_device(): normed_all = lax.all_gather(normed_local, 'vocab', axis=1, tiled=True)  131 us
    pmax x1, blocking collectives, on_device(): maxima = lax.pmax(maxima, 'vocab')  81.8 us
    psum x1, blocking collectives, on_device(): totals, targets = lax.psum((totals, targets), 'vocab')  76.9 us
    dynamic_update_slice x20, other arithmetic, dequantize(): return lax.map(dequantize_group, groups).reshape(height, width)  69.6 us
    reduce_max x40, other arithmetic, dequantize_group(): largest = jnp.max(jnp.abs(blocks), axis=(0, 2), keepdims=True)  37 us
    dot_general x1, matrix products, block_logits(): lax.dot_general(normed_rows, head_rows, (((1,), (1,)), ((), ())), preferr...  17.7 us
  transfers between devices with their start and end apart: 3, of which 3 were waited for; matrix products, arithmetic and copies ran while one was open for 3% of the time, Pallas kernels for 0%

commit v1 on v0

v1 whole, which is shorter than its diff:
```python
import jax
import jax.numpy as jnp
from jax import lax
from jax.experimental import pallas as pl
from jax.experimental.pallas import tpu as pltpu
from jax.sharding import PartitionSpec as P

MESH = pl.DeviceIdType.MESH
QB = 128
f32, bf16, i32 = jnp.float32, jnp.bfloat16, jnp.int32
VOC = 2560
WID = 1792
HALF = WID // 2
D = 7168
MT = 640
HM = VOC // 2 // MT


def remote(src, dst, send_sem, recv_sem, device):
    return pltpu.make_async_remote_copy(
        src_ref=src, dst_ref=dst, send_sem=send_sem, recv_sem=recv_sem, device_id=device, device_id_type=MESH
    )


def kernel(
    h_ref, g_ref, t_ref, w_hbm, e_hbm, logp_ref, emb_ref,
    W, EM, OH, US, UR, TOK, X, PS, PR, ZS, ZR, OWN, PK, RA0, RA1, RB, RC, RD, SD, ST,
    w_sem, e_sem, us_s, us_r, tk_s, tk_r, p1_s, p1_r, p2_s, p2_r, p3_s, p3_r,
    co_s, co_r, z_s, z_r, a_s, a_r, b_s, b_r, c_s, c_r, d_s, d_r, st_s, st_r,
):
    fs, vo = lax.axis_index("fsdp"), lax.axis_index("vocab")
    zh, c = fs // 2, fs % 2
    y, x, zl = vo // 8, (vo // 2) % 4, vo % 2
    z = zh * 2 + zl

    def dev(x_, y_, z_, c_):
        x_, y_, z_, c_ = (x_ + 4) % 4, (y_ + 4) % 4, (z_ + 4) % 4, (c_ + 2) % 2
        return ((z_ // 2) * 2 + c_, (y_ * 4 + x_) * 2 + z_ % 2)

    xs = [(x + d) % 4 for d in range(4)]
    ys = [(y + d) % 4 for d in range(4)]
    column = [(i // 2, i % 2) for i in range(8)]
    ring = (1, 3, 2)
    sends = []

    def go(cp):
        cp.start()
        sends.append(cp)

    w_parts, e_parts = 4, 2
    w_cps = [
        pltpu.make_async_copy(w_hbm.at[pl.ds(i * 640, 640)], W.at[pl.ds(i * 640, 640)], w_sem.at[i])
        for i in range(w_parts)
    ]
    e_cps = [
        pltpu.make_async_copy(e_hbm.at[pl.ds(i * 1280, 1280)], EM.at[pl.ds(i * 1280, 1280)], e_sem.at[i])
        for i in range(e_parts)
    ]
    for cp in w_cps:
        cp.start()
    for cp in e_cps:
        cp.start()

    barrier = pltpu.get_barrier_semaphore()
    peers = [dev(x, y, z + dz, c + dc) for dz, dc in column[1:]]
    peers += [dev(x + d, y, z, c) for d in ring] + [dev(x, y + d, z, c) for d in ring]
    for peer in peers:
        pl.semaphore_signal(barrier, inc=1, device_id=peer, device_id_type=MESH)

    h = jnp.concatenate([h_ref[s].astype(f32) for s in range(4)], axis=0)
    ms = jnp.sum(h * h, axis=1, keepdims=True) * (1.0 / D)
    normed = h * lax.rsqrt(ms + 1e-06) * g_ref[...]
    for q in range(4):
        lo = normed[:, q * WID : q * WID + HALF]
        hi = normed[:, q * WID + HALF : (q + 1) * WID]
        US[q] = jnp.concatenate([lo, hi], axis=0).astype(bf16)
    UR[0] = US[fs]
    TOK[0] = t_ref[...]
    pl.semaphore_wait(barrier, len(peers))

    unit_cps = []
    for i, (dz, dc) in enumerate(column):
        if i == 0:
            continue
        z2, c2 = (z + dz) % 4, (c + dc) % 2
        cp = remote(US.at[(z2 // 2) * 2 + c2], UR.at[i], us_s.at[i], us_r.at[i], dev(x, y, z2, c2))
        go(cp)
        unit_cps.append(cp)
    tok_cps = []
    for i, (dzh, dc) in enumerate(((0, 0), (0, 1), (1, 0), (1, 1))):
        if i == 0:
            continue
        cp = remote(TOK.at[0], TOK.at[i], tk_s.at[i], tk_r.at[i], dev(x, y, z + 2 * dzh, c + dc))
        go(cp)
        tok_cps.append(cp)

    def restore(part):
        w_cps[part].wait()

        def group(n, _):
            rows = pl.ds(pl.multiple_of(part * 640 + n * QB, QB), QB)
            for j in range(WID // QB):
                block = W[rows, j * QB : (j + 1) * QB].astype(f32)
                scale = (jnp.max(jnp.abs(block), axis=(0, 1), keepdims=True) + 1e-06) / 7.0
                coded = jnp.floor(block / scale + 0.5)
                W[rows, j * QB : (j + 1) * QB] = (coded * scale).astype(bf16)
            return 0

        lax.fori_loop(0, 5, group, 0)

    zs = [(1 - zh) * 2, (1 - zh) * 2 + 1, zh * 2, zh * 2 + 1]

    def units():
        for cp in unit_cps:
            cp.wait_recv()
        for k in range(4):
            dz = (z - zs[k] + 4) % 4
            u0 = UR[dz * 2 + c].astype(f32)
            u1 = UR[dz * 2 + (1 - c)].astype(f32)
            X[k, 0, y, x] = jnp.concatenate([u0[:8], u1[:8]], axis=0).astype(bf16)
            X[k, 1, y, x] = jnp.concatenate([u0[8:], u1[8:]], axis=0).astype(bf16)

    def p1_copy(k, n, j, px, py):
        slot = X.at[k, n, py, px]
        target = dev(x + ring[j], y, z, c) if n == 0 else dev(x, y + ring[j], z, c)
        return remote(slot, slot, p1_s.at[k, n, j], p1_r.at[k, n, j], target)

    def p1_send(k):
        for n in range(2):
            for j in range(3):
                go(p1_copy(k, n, j, x, y))

    def p1_wait(k):
        for j in range(3):
            p1_copy(k, 0, j, xs[4 - ring[j]], y).wait_recv()
            p1_copy(k, 1, j, x, ys[4 - ring[j]]).wait_recv()

    def p2_copy(k, n, j, at):
        slot = X.at[k, 0, at] if n == 0 else X.at[k, 1, :, at]
        step = 1 if j == 0 else 3
        target = dev(x, y + step, z, c) if n == 0 else dev(x + step, y, z, c)
        return remote(slot, slot, p2_s.at[k, n, j], p2_r.at[k, n, j], target)

    def p2_send(k):
        for n in range(2):
            for j in range(2):
                go(p2_copy(k, n, j, y if n == 0 else x))

    def p3_copy(k, n, j, at):
        part = pl.ds(0, 2) if j == 0 else pl.ds(2, 2)
        slot = X.at[k, 0, at, part] if n == 0 else X.at[k, 1, part, at]
        step = 1 if j == 0 else 3
        target = dev(x, y + step, z, c) if n == 0 else dev(x + step, y, z, c)
        return remote(slot, slot, p3_s.at[k, n, j], p3_r.at[k, n, j], target)

    def p3_send(k):
        for j in range(2):
            for n in range(2):
                came = (ys if n == 0 else xs)[3 if j == 0 else 1]
                p2_copy(k, n, j, came).wait_recv()
                go(p3_copy(k, n, j, came))

    def p3_wait(k):
        for j in range(2):
            p3_copy(k, 0, j, ys[2]).wait_recv()
            p3_copy(k, 1, j, xs[2]).wait_recv()

    def logits_tile(k, row):
        rhs = jnp.concatenate([X[k, 0].reshape(256, HALF), X[k, 1].reshape(256, HALF)], axis=1)
        rows = pl.ds(pl.multiple_of(row, MT), MT)
        return lax.dot_general(W[rows, :], rhs, (((1,), (1,)), ((), ())), preferred_element_type=f32)

    def core_copy(k, m):
        return remote(PS.at[k, m], PR.at[k, m], co_s.at[k, m], co_r.at[k, m], dev(x, y, z, c + 1))

    def z_copy(k, m):
        return remote(ZS.at[k, m], ZR.at[k, m], z_s.at[k, m], z_r.at[k, m], dev(x, y, z + 2, c))

    def chunk(k):
        def other(m, _):
            PS[k, m] = logits_tile(k, (1 - c) * (HM * MT) + m * MT).astype(bf16)
            core_copy(k, m).start()
            return 0

        def own(m, _):
            part = logits_tile(k, c * (HM * MT) + m * MT)
            core_copy(k, m).wait_recv()
            if k < 2:
                ZS[k, m] = (part + PR[k, m].astype(f32)).astype(bf16)
                z_copy(k, m).start()
            else:
                OWN[k - 2, m] = part + PR[k, m].astype(f32)
            return 0

        lax.fori_loop(0, HM, other, 0)
        lax.fori_loop(0, HM, own, 0)

    def one_hot():
        for cp in tok_cps:
            cp.wait_recv()

        def block(n, _):
            i = ((zh + n // 2) % 2) * 2 + (c + n % 2) % 2
            token = jnp.broadcast_to(TOK[i][0:1].astype(f32), (QB, 256)).T
            first = vo * VOC

            def tile(k, _):
                entry = (lax.broadcasted_iota(i32, (256, QB), 1) + (first + k * QB)).astype(f32)
                OH[pl.ds(pl.multiple_of(n * 256, 256), 256), pl.ds(pl.multiple_of(k * QB, QB), QB)] = jnp.where(
                    token == entry, 1.0, 0.0
                ).astype(bf16)
                return 0

            lax.fori_loop(0, VOC // QB, tile, 0)
            return 0

        lax.fori_loop(0, 4, block, 0)

    def pick(lo, hi):
        def tile(n, _):
            cols = pl.ds(pl.multiple_of(n * 256, 256), 256)
            part = jnp.dot(OH[...], EM[:, cols], preferred_element_type=f32)
            PK[:, :, :, :, cols] = part.astype(bf16).reshape(4, 4, 4, 16, 256)
            return 0

        lax.fori_loop(lo, hi, tile, 0)

    LO, HI = pl.ds(0, HALF), pl.ds(HALF, HALF)

    def a_copy(n, j):
        part = pl.ds(0, 2) if j == 0 else pl.ds(2, 2)
        src = PK.at[ys[2], part, :, :, LO] if n == 0 else PK.at[:, part, xs[2], :, HI]
        step = 1 if j == 0 else 3
        target = dev(x, y + step, z, c) if n == 0 else dev(x + step, y, z, c)
        return remote(src, (RA0 if n == 0 else RA1).at[j], a_s.at[n, j], a_r.at[n, j], target)

    def b_copy(n, j):
        step = 1 if j == 0 else 3
        src = PK.at[ys[step], :, :, :, LO] if n == 0 else PK.at[:, :, xs[step], :, HI]
        target = dev(x, y + step, z, c) if n == 0 else dev(x + step, y, z, c)
        return remote(src, RB.at[n, j], b_s.at[n, j], b_r.at[n, j], target)

    def c_copy(n, j):
        src = PK.at[y, :, xs[ring[j]], :, LO] if n == 0 else PK.at[ys[ring[j]], :, x, :, HI]
        target = dev(x + ring[j], y, z, c) if n == 0 else dev(x, y + ring[j], z, c)
        return remote(src, RC.at[n, j], c_s.at[n, j], c_r.at[n, j], target)

    def a_send():
        for n in range(2):
            for j in range(2):
                go(a_copy(n, j))

    def b_send():
        for j in range(2):
            step = 1 if j == 0 else 3
            for n in range(2):
                a_copy(n, j).wait_recv()
                for s in range(2):
                    if n == 0:
                        PK[ys[step], 2 * j + s, :, :, LO] = PK[ys[step], 2 * j + s, :, :, LO] + RA0[j, s]
                    else:
                        PK[:, 2 * j + s, xs[step], :, HI] = PK[:, 2 * j + s, xs[step], :, HI] + RA1[j, :, s]
                go(b_copy(n, j))

    def c_send():
        for n in range(2):
            for j in range(2):
                b_copy(n, j).wait_recv()
            for s in range(4):
                if n == 0:
                    PK[y, s, :, :, LO] = PK[y, s, :, :, LO] + (RB[0, 0, s] + RB[0, 1, s])
                else:
                    PK[:, s, x, :, HI] = PK[:, s, x, :, HI] + (RB[1, 0, :, s] + RB[1, 1, :, s])
            for j in range(3):
                go(c_copy(n, j))

    d_copy = remote(SD, RD, d_s, d_r, dev(x, y, zh * 2 + (1 - zl), c))

    def d_send():
        total = []
        for n in range(2):
            for j in range(3):
                c_copy(n, j).wait_recv()
            cols = LO if n == 0 else HI
            total.append(PK[y, :, x, :, cols] + (RC[n, 0] + RC[n, 1] + RC[n, 2]))
        total = jnp.concatenate(total, axis=2).astype(f32)
        first, second = total[:, :8, :].reshape(32, WID), total[:, 8:, :].reshape(32, WID)
        mine = zl == 0
        SD[...] = jnp.where(mine, second, first).astype(bf16)
        go(d_copy)
        return jnp.where(mine, first, second)

    def d_done(kept):
        d_copy.wait_recv()
        rows = kept + RD[...].astype(f32)
        for s in range(4):
            emb_ref[s] = rows[s * 8 : (s + 1) * 8].astype(bf16)

    def stats(k):
        token = TOK[0][1 + k : 2 + k] + TOK[1][1 + k : 2 + k]

        def tile(m, carry):
            top, total, target = carry
            z_copy(k, m).wait_recv()
            logits = OWN[k, m] + ZR[k, m].astype(f32)
            entry = lax.broadcasted_iota(i32, (MT, 256), 0) + (vo * VOC + c * (HM * MT) + m * MT)
            target = target + jnp.sum(jnp.where(entry == token, logits, 0.0).reshape(MT // 8, 8, 256), axis=0)
            new = jnp.maximum(top, jnp.max(logits.reshape(MT // 8, 8, 256), axis=0))
            part = jnp.sum(jnp.exp(logits.reshape(MT // 8, 8, 256) - new[None]), axis=0)
            return new, total * jnp.exp(top - new) + part, target

        start = (jnp.full((8, 256), -3e38, f32), jnp.zeros((8, 256), f32), jnp.zeros((8, 256), f32))
        top, total, target = lax.fori_loop(0, HM, tile, start)
        new = jnp.max(top, axis=0, keepdims=True)
        total = jnp.sum(total * jnp.exp(top - new), axis=0, keepdims=True)
        return new, total, jnp.sum(target, axis=0, keepdims=True)

    def combine():
        a, b = stats(0), stats(1)
        top, total, target = (jnp.concatenate([p, q], axis=0) for p, q in zip(a, b))
        for stage in range(3):
            ST[stage, 0] = jnp.concatenate([top, total, target, jnp.zeros((2, 256), f32)], axis=0)
            targets = (
                [dev(x, y, z, c + 1), dev(x, y, zh * 2 + 1 - zl, c), dev(x, y, zh * 2 + 1 - zl, c + 1)],
                [dev(x + d, y, z, c) for d in ring],
                [dev(x, y + d, z, c) for d in ring],
            )[stage]
            cps = [
                remote(ST.at[stage, 0], ST.at[stage, 1 + j], st_s.at[stage, j], st_r.at[stage, j], targets[j])
                for j in range(3)
            ]
            for cp in cps:
                go(cp)
            for cp in cps:
                cp.wait_recv()
            got = [ST[stage, j] for j in range(4)]
            tops = [g[0:2] for g in got]
            top = jnp.maximum(jnp.maximum(tops[0], tops[1]), jnp.maximum(tops[2], tops[3]))
            total = sum(g[2:4] * jnp.exp(t - top) for g, t in zip(got, tops))
            target = sum(g[4:6] for g in got)
        logp_ref[...] = jnp.concatenate([target - top - jnp.log(total), jnp.zeros((6, 256), f32)], axis=0)

    restore(0)
    restore(1)
    units()
    p1_send(0)
    p1_send(1)
    restore(2)
    p1_wait(0)
    p2_send(0)
    restore(3)
    p1_wait(1)
    p2_send(1)
    one_hot()
    p3_send(0)
    p1_send(2)
    for cp in e_cps:
        cp.wait()
    pick(0, 1)
    p3_wait(0)
    chunk(0)
    p3_send(1)
    p1_send(3)
    pick(1, 3)
    p3_wait(1)
    chunk(1)
    pick(3, 7)
    a_send()
    p1_wait(2)
    p2_send(2)
    b_send()
    p3_send(2)
    p1_wait(3)
    p2_send(3)
    p3_wait(2)
    chunk(2)
    c_send()
    p3_send(3)
    p3_wait(3)
    chunk(3)
    kept = d_send()
    d_done(kept)
    combine()
    for k in range(4):
        for m in range(HM):
            core_copy(k, m).wait_send()
            if k < 2:
                z_copy(k, m).wait_send()
    for cp in sends:
        cp.wait_send()


def on_device(head_table, embed_table, hidden, norm_gain, tokens):
    core = lax.axis_index("fsdp") % 2
    plain = tokens.reshape(1, 256)
    by_place = tokens.reshape(4, 16, 2, 2).transpose(2, 1, 0, 3).reshape(2, 16, 1, 8)
    mine = lax.broadcasted_iota(i32, (1, 1, 2, 1), 2) == core
    placed = jnp.where(mine, by_place, 0).reshape(2, 256)
    table = jnp.concatenate([plain, placed, jnp.zeros((5, 256), i32)], axis=0)

    dma = pltpu.SemaphoreType.DMA
    pairs = ((8,), (4,), (4, 2, 3), (4, 2, 2), (4, 2, 2), (4, HM), (2, HM), (2, 2), (2, 2), (2, 3), (), (3, 3))
    sems = []
    for shape in pairs:
        sems += [dma(shape) if shape else dma] * 2
    vm, hbm = pl.BlockSpec(memory_space=pltpu.VMEM), pl.BlockSpec(memory_space=pl.ANY)
    logp, emb = pl.pallas_call(
        kernel,
        name="head",
        out_shape=(jax.ShapeDtypeStruct((8, 256), f32), jax.ShapeDtypeStruct((4, 8, WID), bf16)),
        in_specs=[vm, vm, vm, hbm, hbm],
        out_specs=(vm, vm),
        scratch_shapes=[
            pltpu.VMEM((VOC, WID), bf16),
            pltpu.VMEM((VOC, WID), bf16),
            pltpu.VMEM((1024, VOC), bf16),
            pltpu.VMEM((4, 16, HALF), bf16),
            pltpu.VMEM((8, 16, HALF), bf16),
            pltpu.VMEM((4, 8, 256), i32),
            pltpu.VMEM((4, 2, 4, 4, 16, HALF), bf16),
            pltpu.VMEM((4, HM, MT, 256), bf16),
            pltpu.VMEM((4, HM, MT, 256), bf16),
            pltpu.VMEM((2, HM, MT, 256), bf16),
            pltpu.VMEM((2, HM, MT, 256), bf16),
            pltpu.VMEM((2, HM, MT, 256), f32),
            pltpu.VMEM((4, 4, 4, 16, WID), bf16),
            pltpu.VMEM((2, 2, 4, 16, HALF), bf16),
            pltpu.VMEM((2, 4, 2, 16, HALF), bf16),
            pltpu.VMEM((2, 2, 4, 4, 16, HALF), bf16),
            pltpu.VMEM((2, 3, 4, 16, HALF), bf16),
            pltpu.VMEM((32, WID), bf16),
            pltpu.VMEM((32, WID), bf16),
            pltpu.VMEM((3, 4, 8, 256), f32),
            dma((4,)),
            dma((2,)),
            *sems,
        ],
        compiler_params=pltpu.CompilerParams(
            collective_id=0, has_side_effects=True, vmem_limit_bytes=62 * 2**20
        ),
    )(hidden, norm_gain.reshape(1, D), table, head_table, embed_table)
    rows = logp[:2].reshape(2, 16, 2, 4, 2)
    rows = jnp.where(core == 0, rows[:, :, 0], rows[:, :, 1])
    logprobs = rows.transpose(2, 1, 0, 3).reshape(4, 64)
    return (logprobs, emb)


def solution(mesh):
    placed = (
        P("vocab", "fsdp"),
        P("vocab", "fsdp"),
        P(None, ("fsdp", "vocab"), None),
        P(),
        P(None, "fsdp"),
    )
    return jax.shard_map(
        on_device,
        mesh=mesh,
        in_specs=placed,
        out_specs=(P(None, "fsdp"), P(None, "vocab", "fsdp")),
        check_vma=False,
    )
```

time: 858 us -> 108 us (0.13)
  waiting for transfers between devices: 519 us -> 0 us
  blocking collectives: 166 us -> 0 us
  other arithmetic: 113 us -> 0.7 us
  Pallas kernels: 0 us -> 101 us
  local copies, waits for them, and re-layouts: 27 us -> 5.49 us
  matrix products: 17.7 us -> 0 us
  between operations: 13.8 us -> 0.7 us
    all_gather x2 -> x0, waiting for transfers between devices: 353 us -> none  [the longest x1 222 us: on_device(): head_rows = lax.all_gather(head_table, 'fsdp', axis=1, tiled=True)]
    unnamed x4 -> x0, waiting for transfers between devices: 166 us -> none
    pallas_call x0 -> x1, Pallas kernels: none -> 101 us  [on_device(): pl.pallas_call(kernel, name='head', out_shape=(jax.ShapeDtypeStruct((8, 2...]
    pmax x1 -> x0, blocking collectives: 81.8 us -> none  [on_device(): maxima = lax.pmax(maxima, 'vocab')]
    psum x1 -> x0, blocking collectives: 76.9 us -> none  [on_device(): totals, targets = lax.psum((totals, targets), 'vocab')]
    dynamic_update_slice x20 -> x0, other arithmetic: 69.6 us -> none  [dequantize(): return lax.map(dequantize_group, groups).reshape(height, width)]
    reduce_max x40 -> x0, other arithmetic: 37 us -> none  [dequantize_group(): largest = jnp.max(jnp.abs(blocks), axis=(0, 2), keepdims=True)]
    dot_general x1 -> x0, matrix products: 17.7 us -> none  [block_logits(): lax.dot_general(normed_rows, head_rows, (((1,), (1,)), ((), ())), preferr...]
  transfers between devices with their start and end apart: 3 -> 0, of which waited for: 3 -> 0; matrix products, arithmetic and copies ran while one was open for 3% -> 0% of each run, Pallas kernels for 0% -> 0%
where the time goes in v1:
time: 108 us
  Pallas kernels  101 us (94%)
  local copies, waits for them, and re-layouts  5.49 us (5%)
    pallas_call x1, Pallas kernels, on_device(): pl.pallas_call(kernel, name='head', out_shape=(jax.ShapeDtypeStruct((8, 2...  101 us
    unnamed x3, local copies, waits for them, and re-layouts  2.98 us

profile of v1, /device:TPU:0, one launch (start us, length us, event | category | flops | bytes accessed | tf_op | source)
XLA Modules:
  0.0 108.0 jit_solution(6334299971485577496)
XLA Ops:
  0.7 0.1 pad.2.clone
  0.7 0.8 reshape.32
  1.5 0.1 broadcast_in_dim.31
  1.6 0.1 broadcast_in_dim.32
  1.7 0.8 copy.8
  2.5 0.1 copy.9
  2.6 0.1 copy.10
  2.7 0.1 broadcast_in_dim.36
  2.8 0.7 add_add_fusion.t_ref
  3.4 101.1 %head.1 = (f32[8,256]{1,0:T(8,128)}, bf16[4,8,1792]{2,1,0:T(8,128)(2,1)}) custom-call(bf16[4,2,7168]{2,1,0:T(2,128)(2,1)} %h_ref.1, f32[1,7168]{1,0:T(1,128)} %bitcast.13, s32[8,256]{1,0:T(8,128)} %add_add_fusion.t_ref, bf16[2560,1792]{1,0:T(8,128)(2,1)} %w_hbm.1, bf16[2560,1792]{1,0:T(8,128)(2,1)} %e_hbm.1), custom_call_target="tpu_custom_call" | custom-call | tf_op jit(solution)/shard_map/head/pallas_call | solution.py:407
  104.6 0.7 slice.9
  105.3 0.2 reshape.34
  105.5 0.3 copy.11
  105.8 0.7 copy.12
  106.5 1.6 %copy.14 = bf16[4,8,1792]{2,1,0:T(8,128)(2,1)} copy(bf16[4,8,1792]{2,1,0:T(8,128)(2,1)} %get-tuple-element.11) | data formatting | bytes 229376
  (5 shorter events, 0.1 us)

commit v2 on v1

v2 whole, which is shorter than its diff:
```python
import functools

import jax
import jax.numpy as jnp
from jax import lax
from jax.experimental import pallas as pl
from jax.experimental.pallas import tpu as pltpu
from jax.sharding import PartitionSpec as P

MESH = pl.DeviceIdType.MESH
QB = 128
f32, bf16, i32 = jnp.float32, jnp.bfloat16, jnp.int32
VOC = 2560
WID = 1792
HALF = WID // 2
D = 7168
MT = 640
HM = VOC // 2 // MT
ZT = 320
HZ = VOC // 2 // ZT
LOW, HIGH = 1024, 768
DIRECT = (0,)


def remote(src, dst, send_sem, recv_sem, device):
    return pltpu.make_async_remote_copy(
        src_ref=src, dst_ref=dst, send_sem=send_sem, recv_sem=recv_sem, device_id=device, device_id_type=MESH
    )


def kernel(
    h_ref, g_ref, t_ref, w_hbm, e_hbm, logp_ref, emb_ref,
    W, EM, OH, US, UR, TOK, PERM, X, PS, PR, ZS, ZR, OWN, PK, RA0, RA1, RB0, RB1, RC0, RC1, RD, SD, SA, SB,
    w_sem, e_sem, us_s, us_r, tk_s, tk_r, p1_s, p1_r, p2_s, p2_r, p3_s, p3_r,
    co_s, co_r, z_s, z_r, a_s, a_r, b_s, b_r, c_s, c_r, d_s, d_r, sa_s, sa_r, sb_s, sb_r,
):
    fs, vo = lax.axis_index("fsdp"), lax.axis_index("vocab")
    zh, c = fs // 2, fs % 2
    y, x, zl = vo // 8, (vo // 2) % 4, vo % 2
    z = zh * 2 + zl
    zn = zh * 2 + 1 - zl

    def dev(x_, y_, z_, c_):
        x_, y_, z_, c_ = (x_ + 4) % 4, (y_ + 4) % 4, (z_ + 4) % 4, (c_ + 2) % 2
        return ((z_ // 2) * 2 + c_, (y_ * 4 + x_) * 2 + z_ % 2)

    xs = [(x + d) % 4 for d in range(4)]
    ys = [(y + d) % 4 for d in range(4)]
    column = [(i // 2, i % 2) for i in range(8)]
    plane = [(i % 4, i // 4) for i in range(16)]
    ring = (1, 3, 2)
    sends = []

    def go(cp):
        cp.start()
        sends.append(cp)

    w_cps = [
        pltpu.make_async_copy(w_hbm.at[pl.ds(i * 640, 640)], W.at[pl.ds(i * 640, 640)], w_sem.at[i])
        for i in range(4)
    ]
    e_cps = [
        pltpu.make_async_copy(e_hbm.at[pl.ds(i * 1280, 1280)], EM.at[pl.ds(i * 1280, 1280)], e_sem.at[i])
        for i in range(2)
    ]
    for cp in w_cps[:2] + e_cps + w_cps[2:]:
        cp.start()

    barrier = pltpu.get_barrier_semaphore()
    peers = [dev(x, y, z + dz, c + dc) for dz, dc in column[1:]]
    peers += [dev(x + dx, y + dy, z, c) for dx, dy in plane[1:]]
    for peer in peers:
        pl.semaphore_signal(barrier, inc=1, device_id=peer, device_id_type=MESH)

    h = jnp.concatenate([h_ref[s].astype(f32) for s in range(4)], axis=0)
    ms = jnp.sum(h * h, axis=1, keepdims=True) * (1.0 / D)
    normed = h * lax.rsqrt(ms + 1e-06) * g_ref[...]
    for q in range(4):
        lo = normed[:, q * WID : q * WID + HALF]
        hi = normed[:, q * WID + HALF : (q + 1) * WID]
        US[q] = jnp.concatenate([lo, hi], axis=0).astype(bf16)
    UR[0] = US[fs]

    k_ = lax.broadcasted_iota(i32, (256, 512), 0)
    l_ = lax.broadcasted_iota(i32, (256, 512), 1)
    given = ((l_ >> 1) & 3) * 64 + ((l_ >> 4) & 15) * 4 + (l_ >> 8) * 2 + (l_ & 1)
    PERM[...] = jnp.where((k_ == given) & (((l_ >> 3) & 1) == c), 1.0, 0.0).astype(bf16)
    t = t_ref[...].astype(f32)
    plain = jnp.concatenate([t[s : s + 1] for s in range(4)], axis=1)
    top_part = jnp.floor(plain * (1.0 / 16384.0))
    mid_part = jnp.floor((plain - top_part * 16384.0) * (1.0 / 128.0))
    low_part = plain - top_part * 16384.0 - mid_part * 128.0
    parts = jnp.concatenate([top_part, mid_part, low_part, jnp.zeros((5, 256), f32)], axis=0).astype(bf16)
    moved = jnp.dot(parts, PERM[...], preferred_element_type=f32)
    placed = moved[0:1] * 16384.0 + moved[1:2] * 128.0 + moved[2:3]
    TOK[0] = jnp.concatenate([plain, placed[:, :256], placed[:, 256:], jnp.zeros((5, 256), f32)], axis=0)

    pl.semaphore_wait(barrier, len(peers))

    unit_cps = []
    for i, (dz, dc) in enumerate(column):
        z2, c2 = (z + dz) % 4, (c + dc) % 2
        if i:
            unit_cps.append(
                remote(US.at[(z2 // 2) * 2 + c2], UR.at[i], us_s.at[i], us_r.at[i], dev(x, y, z2, c2))
            )
    tok_cps = [
        remote(TOK.at[0], TOK.at[i], tk_s.at[i], tk_r.at[i], dev(x, y, z + 2 * (i // 2), c + i % 2))
        for i in range(1, 4)
    ]
    for cp in unit_cps[:1] + tok_cps + unit_cps[1:]:
        go(cp)

    def restore(part):
        w_cps[part].wait()

        def group(n, _):
            rows = pl.ds(pl.multiple_of(part * 640 + n * QB, QB), QB)
            for j in range(WID // QB):
                block = W[rows, j * QB : (j + 1) * QB].astype(f32)
                scale = (jnp.max(jnp.abs(block), axis=(0, 1), keepdims=True) + 1e-06) / 7.0
                coded = jnp.floor(block / scale + 0.5)
                W[rows, j * QB : (j + 1) * QB] = (coded * scale).astype(bf16)
            return 0

        lax.fori_loop(0, 5, group, 0)

    zs = [z, zn, (z + 2) % 4, (zn + 2) % 4]

    def units(ks):
        for k in ks:
            dz = (z - zs[k] + 4) % 4
            u0 = UR[dz * 2 + c].astype(f32)
            u1 = UR[dz * 2 + (1 - c)].astype(f32)
            X[k, 0, y, x] = jnp.concatenate([u0[:8], u1[:8]], axis=0).astype(bf16)
            X[k, 1, y, x] = jnp.concatenate([u0[8:], u1[8:]], axis=0).astype(bf16)

    def first_unit():
        unit_cps[0].wait_recv()
        units((0,))

    def other_units():
        for cp in unit_cps[1:]:
            cp.wait_recv()
        units((1, 2, 3))

    def p1_copy(k, n, j, px, py):
        slot = X.at[k, n, py, px]
        target = dev(x + ring[j], y, z, c) if n == 0 else dev(x, y + ring[j], z, c)
        return remote(slot, slot, p1_s.at[k, n, j], p1_r.at[k, n, j], target)

    def p1_send(k):
        for j in range(3):
            for n in range(2):
                go(p1_copy(k, n, j, x, y))

    def p1_wait(k):
        for j in range(3):
            p1_copy(k, 0, j, xs[4 - ring[j]], y).wait_recv()
            p1_copy(k, 1, j, x, ys[4 - ring[j]]).wait_recv()

    def p2_copy(k, n, j, at):
        slot = X.at[k, 0, at] if n == 0 else X.at[k, 1, :, at]
        target = dev(x, y + ring[j], z, c) if n == 0 else dev(x + ring[j], y, z, c)
        return remote(slot, slot, p2_s.at[k, n, j], p2_r.at[k, n, j], target)

    def p2_send(k):
        for j in range(3 if k in DIRECT else 2):
            for n in range(2):
                go(p2_copy(k, n, j, y if n == 0 else x))

    def p3_copy(k, n, j, at):
        part = pl.ds(0, 2) if j == 0 else pl.ds(2, 2)
        slot = X.at[k, 0, at, part] if n == 0 else X.at[k, 1, part, at]
        target = dev(x, y + ring[j], z, c) if n == 0 else dev(x + ring[j], y, z, c)
        return remote(slot, slot, p3_s.at[k, n, j], p3_r.at[k, n, j], target)

    def p2_wait(k, n, j):
        came = (ys if n == 0 else xs)[4 - ring[j]]
        p2_copy(k, n, j, came).wait_recv()
        return came

    def p3_send(k):
        for j in range(2):
            for n in range(2):
                go(p3_copy(k, n, j, p2_wait(k, n, j)))

    def gathered(k):
        if k in DIRECT:
            for j in range(3):
                for n in range(2):
                    p2_wait(k, n, j)
        else:
            for j in range(2):
                p3_copy(k, 0, j, ys[2]).wait_recv()
                p3_copy(k, 1, j, xs[2]).wait_recv()

    def logits_tile(k, row):
        rhs = jnp.concatenate([X[k, 0].reshape(256, HALF), X[k, 1].reshape(256, HALF)], axis=1)
        rows = pl.ds(pl.multiple_of(row, MT), MT)
        return lax.dot_general(W[rows, :], rhs, (((1,), (1,)), ((), ())), preferred_element_type=f32)

    def core_copy(k, m):
        return remote(PS.at[k, m], PR.at[k, m], co_s.at[k, m], co_r.at[k, m], dev(x, y, z, c + 1))

    def z_copy(k, m):
        return remote(ZS.at[k, m], ZR.at[k, m], z_s.at[k, m], z_r.at[k, m], dev(x, y, z + 2, c))

    def chunk(k):
        def other(m, _):
            PS[k, m] = logits_tile(k, (1 - c) * (HM * MT) + m * MT).astype(bf16)
            core_copy(k, m).start()
            return 0

        def own(m, _):
            part = logits_tile(k, c * (HM * MT) + m * MT)
            core_copy(k, m).wait_recv()
            both = (part + PR[k, m].astype(f32)).reshape(MT // ZT, ZT, 256)
            here = pl.ds(m * (MT // ZT), MT // ZT)
            if k < 2:
                ZS[k, here] = both.astype(bf16)
                for i in range(MT // ZT):
                    z_copy(k, m * (MT // ZT) + i).start()
            else:
                OWN[k - 2, here] = both
            return 0

        lax.fori_loop(0, HM, other, 0)
        lax.fori_loop(0, HM, own, 0)

    def one_hot():
        for cp in tok_cps:
            cp.wait_recv()

        def block(n, _):
            of = (y + n + 2) % 4
            i = ((zh + of // 2) % 2) * 2 + (c + of % 2) % 2
            token = jnp.broadcast_to(TOK[i][0:1], (QB, 256)).T
            first = vo * VOC

            def tile(k, _):
                entry = (lax.broadcasted_iota(i32, (256, QB), 1) + (first + k * QB)).astype(f32)
                hot = jnp.where(token == entry, 1.0, 0.0).astype(bf16).reshape(4, 4, 16, QB)
                for px in range(4):
                    OH[n, :, (px - x + 6) % 4, :, pl.ds(pl.multiple_of(k * QB, QB), QB)] = hot[:, px]
                return 0

            lax.fori_loop(0, VOC // QB, tile, 0)
            return 0

        lax.fori_loop(0, 4, block, 0)

    def pick(n, first, lo, hi):
        part = pl.ds(0, 1) if first else pl.ds(1, 3)
        slots = 1 if first else 3

        def tile(i, _):
            cols = pl.ds(pl.multiple_of(n * LOW + i * 256, 256), 256)
            hot = OH[part] if n == 0 else OH[:, :, part]
            got = jnp.dot(hot.reshape(slots * 256, VOC), EM[:, cols], preferred_element_type=f32).astype(bf16)
            if n == 0:
                PK[part, :, :, :, cols] = got.reshape(slots, 4, 4, 16, 256)
            else:
                PK[:, :, part, :, cols] = got.reshape(4, 4, slots, 16, 256)
            return 0

        lax.fori_loop(lo, hi, tile, 0)

    LO, HI = pl.ds(0, LOW), pl.ds(LOW, HIGH)

    def along(n, d):
        return dev(x, y + d, z, c) if n == 0 else dev(x + d, y, z, c)

    def a_copy(n, j):
        part = pl.ds(2 * j, 2)
        src = PK.at[0, part, :, :, LO] if n == 0 else PK.at[:, part, 0, :, HI]
        return remote(src, (RA0 if n == 0 else RA1).at[j], a_s.at[n, j], a_r.at[n, j], along(n, ring[j]))

    def b_copy(n, j):
        slot = 3 - 2 * j
        src = PK.at[slot, :, :, :, LO] if n == 0 else PK.at[:, :, slot, :, HI]
        return remote(src, (RB0 if n == 0 else RB1).at[j], b_s.at[n, j], b_r.at[n, j], along(n, ring[j]))

    def c_copy(n, j):
        slot = (ring[j] + 2) % 4
        src = PK.at[2, :, slot, :, LO] if n == 0 else PK.at[slot, :, 2, :, HI]
        return remote(src, (RC0 if n == 0 else RC1).at[j], c_s.at[n, j], c_r.at[n, j], along(1 - n, ring[j]))

    def a_send(n):
        for j in range(2):
            go(a_copy(n, j))

    def b_send(n):
        for j in range(2):
            slot = 3 - 2 * j
            a_copy(n, j).wait_recv()
            for s in range(2):
                if n == 0:
                    PK[slot, 2 * j + s, :, :, LO] = PK[slot, 2 * j + s, :, :, LO] + RA0[j, s]
                else:
                    PK[:, 2 * j + s, slot, :, HI] = PK[:, 2 * j + s, slot, :, HI] + RA1[j, :, s]
            go(b_copy(n, j))

    def c_send(n):
        for j in range(2):
            b_copy(n, j).wait_recv()
        for s in range(4):
            if n == 0:
                PK[2, s, :, :, LO] = PK[2, s, :, :, LO] + (RB0[0, s] + RB0[1, s])
            else:
                PK[:, s, 2, :, HI] = PK[:, s, 2, :, HI] + (RB1[0, :, s] + RB1[1, :, s])
        for j in range(3):
            go(c_copy(n, j))

    d_copy = remote(SD, RD, d_s, d_r, dev(x, y, zn, c))

    def d_send():
        total = []
        for n in range(2):
            for j in range(3):
                c_copy(n, j).wait_recv()
            got = RC0 if n == 0 else RC1
            total.append(PK[2, :, 2, :, LO if n == 0 else HI] + (got[0] + got[1] + got[2]))
        total = jnp.concatenate(total, axis=2).astype(f32)
        first, second = total[:, :8, :].reshape(32, WID), total[:, 8:, :].reshape(32, WID)
        mine = zl == 0
        SD[...] = jnp.where(mine, second, first).astype(bf16)
        go(d_copy)
        return jnp.where(mine, first, second)

    def d_done(kept):
        d_copy.wait_recv()
        rows = kept + RD[...].astype(f32)
        for s in range(4):
            emb_ref[s] = rows[s * 8 : (s + 1) * 8].astype(bf16)

    def stats(k):
        place = zl if k == 0 else 1 - zl
        token = (TOK[2] + TOK[3])[1:3]
        token = jnp.where(place == 0, token[0:1], token[1:2])

        def tile(m, carry):
            top, total, target = carry
            z_copy(k, m).wait_recv()
            logits = (OWN[k, m] + ZR[k, m].astype(f32)).reshape(ZT // 8, 8, 256)
            entry = lax.broadcasted_iota(i32, (ZT, 256), 0) + (vo * VOC + c * (HM * MT) + m * ZT)
            hit = (entry.astype(f32) == token).reshape(ZT // 8, 8, 256)
            target = target + jnp.sum(jnp.where(hit, logits, 0.0), axis=0)
            new = jnp.maximum(top, jnp.max(logits, axis=0))
            part = jnp.sum(jnp.exp(logits - new[None]), axis=0)
            return new, total * jnp.exp(top - new) + part, target

        start = (jnp.full((8, 256), -3e38, f32), jnp.zeros((8, 256), f32), jnp.zeros((8, 256), f32))
        top, total, target = lax.fori_loop(0, HZ, tile, start)
        new = jnp.max(top, axis=0, keepdims=True)
        total = jnp.sum(total * jnp.exp(top - new), axis=0, keepdims=True)
        return new, total, jnp.sum(target, axis=0, keepdims=True)

    def merge(got):
        tops = [g[0:2] for g in got]
        top = functools.reduce(jnp.maximum, tops)
        total = sum(g[2:4] * jnp.exp(t - top) for g, t in zip(got, tops))
        return top, total, sum(g[4:6] for g in got)

    pad = jnp.zeros((2, 256), f32)
    first_targets = [dev(x, y, z_ + 2, c_) for z_ in (z, zn) for c_ in (c, c + 1)]

    def first_copy(j):
        return remote(SA.at[0], SA.at[1 + j], sa_s.at[j], sa_r.at[j], first_targets[j])

    def second_copy(i):
        return remote(SB.at[0], SB.at[i], sb_s.at[i], sb_r.at[i], dev(x + plane[i][0], y + plane[i][1], z, c))

    def first_send(a, b):
        got = [jnp.concatenate(p, axis=0) for p in zip(a, b)]
        got = [jnp.where(zl == 0, g, jnp.concatenate([g[1:2], g[0:1]], axis=0)) for g in got]
        SA[0] = jnp.concatenate([*got, pad], axis=0)
        for j in range(4):
            go(first_copy(j))

    def second_send():
        for j in range(4):
            first_copy(j).wait_recv()
        SB[0] = jnp.concatenate([*merge([SA[1 + j] for j in range(4)]), pad], axis=0)
        for i in range(1, 16):
            go(second_copy(i))

    def finish():
        for i in range(1, 16):
            second_copy(i).wait_recv()
        top, total, target = merge([SB[i] for i in range(16)])
        logp = target - top - jnp.log(total)
        logp = jnp.concatenate([logp[0:1], logp[1:2]], axis=1)
        one = logp.astype(bf16)
        two = (logp - one.astype(f32)).astype(bf16)
        three = (logp - one.astype(f32) - two.astype(f32)).astype(bf16)
        parts = jnp.concatenate(
            [one.astype(f32), two.astype(f32), three.astype(f32), jnp.zeros((5, 512), f32)], axis=0
        ).astype(bf16)
        moved = lax.dot_general(parts, PERM[...], (((1,), (1,)), ((), ())), preferred_element_type=f32)
        row = moved[0:1] + moved[1:2] + moved[2:3]
        logp_ref[...] = jnp.concatenate([row[:, 64 * s : 64 * (s + 1)] for s in range(4)], axis=0)

    restore(0)
    first_unit()
    p1_send(0)
    restore(1)
    one_hot()
    p1_wait(0)
    p2_send(0)
    for cp in e_cps:
        cp.wait()
    pick(0, True, 0, 4)
    a_send(0)
    other_units()
    p1_send(1)
    p1_send(2)
    p1_send(3)
    pick(1, True, 0, 3)
    a_send(1)
    restore(2)
    restore(3)
    p1_wait(1)
    p2_send(1)
    gathered(0)
    chunk(0)
    p1_wait(2)
    p1_wait(3)
    p2_send(2)
    p2_send(3)
    pick(0, False, 0, 4)
    p3_send(1)
    b_send(0)
    pick(1, False, 0, 3)
    b_send(1)
    p3_send(2)
    p3_send(3)
    gathered(1)
    chunk(1)
    c_send(0)
    c_send(1)
    gathered(2)
    chunk(2)
    gathered(3)
    chunk(3)
    early = stats(0)
    kept = d_send()
    first_send(early, stats(1))
    d_done(kept)
    second_send()
    finish()
    for k in range(4):
        for m in range(HM):
            core_copy(k, m).wait_send()
    for k in range(2):
        for m in range(HZ):
            z_copy(k, m).wait_send()
    for cp in sends:
        cp.wait_send()


def hand_over(logp_ref, emb_ref, logp_out, emb_out):
    logp_out[...] = logp_ref[...]
    emb_out[...] = emb_ref[...]


def on_device(head_table, embed_table, hidden, norm_gain, tokens):
    dma = pltpu.SemaphoreType.DMA
    pairs = ((8,), (4,), (4, 2, 3), (4, 2, 3), (4, 2, 2), (4, HM), (2, HZ), (2, 2), (2, 2), (2, 3), (), (4,), (16,))
    sems = []
    for shape in pairs:
        sems += [dma(shape) if shape else dma] * 2
    vm, hbm = pl.BlockSpec(memory_space=pltpu.VMEM), pl.BlockSpec(memory_space=pl.ANY)
    logp, emb = pl.pallas_call(
        kernel,
        name="head",
        out_shape=(jax.ShapeDtypeStruct((4, 64), f32), jax.ShapeDtypeStruct((4, 8, WID), bf16)),
        in_specs=[vm, vm, vm, hbm, hbm],
        out_specs=(vm, vm),
        scratch_shapes=[
            pltpu.VMEM((VOC, WID), bf16),
            pltpu.VMEM((VOC, WID), bf16),
            pltpu.VMEM((4, 4, 4, 16, VOC), bf16),
            pltpu.VMEM((4, 16, HALF), bf16),
            pltpu.VMEM((8, 16, HALF), bf16),
            pltpu.VMEM((4, 8, 256), f32),
            pltpu.VMEM((256, 512), bf16),
            pltpu.VMEM((4, 2, 4, 4, 16, HALF), bf16),
            pltpu.VMEM((4, HM, MT, 256), bf16),
            pltpu.VMEM((4, HM, MT, 256), bf16),
            pltpu.VMEM((2, HZ, ZT, 256), bf16),
            pltpu.VMEM((2, HZ, ZT, 256), bf16),
            pltpu.VMEM((2, HZ, ZT, 256), f32),
            pltpu.VMEM((4, 4, 4, 16, WID), bf16),
            pltpu.VMEM((2, 2, 4, 16, LOW), bf16),
            pltpu.VMEM((2, 4, 2, 16, HIGH), bf16),
            pltpu.VMEM((2, 4, 4, 16, LOW), bf16),
            pltpu.VMEM((2, 4, 4, 16, HIGH), bf16),
            pltpu.VMEM((3, 4, 16, LOW), bf16),
            pltpu.VMEM((3, 4, 16, HIGH), bf16),
            pltpu.VMEM((32, WID), bf16),
            pltpu.VMEM((32, WID), bf16),
            pltpu.VMEM((5, 8, 256), f32),
            pltpu.VMEM((16, 8, 256), f32),
            dma((4,)),
            dma((2,)),
            *sems,
        ],
        compiler_params=pltpu.CompilerParams(
            collective_id=0, has_side_effects=True, vmem_limit_bytes=62 * 2**20
        ),
    )(hidden, norm_gain.reshape(1, D), tokens, head_table, embed_table)
    return pl.pallas_call(
        hand_over,
        name="results",
        out_shape=(jax.ShapeDtypeStruct((4, 64), f32), jax.ShapeDtypeStruct((4, 8, WID), bf16)),
        in_specs=[vm, vm],
        out_specs=(vm, vm),
    )(logp, emb)


def solution(mesh):
    placed = (
        P("vocab", "fsdp"),
        P("vocab", "fsdp"),
        P(None, ("fsdp", "vocab"), None),
        P(),
        P(None, "fsdp"),
    )
    return jax.shard_map(
        on_device,
        mesh=mesh,
        in_specs=placed,
        out_specs=(P(None, "fsdp"), P(None, "vocab", "fsdp")),
        check_vma=False,
    )
```

time: 108 us -> 79.5 us (0.74)
  Pallas kernels: 101 us -> 78.5 us
  local copies, waits for them, and re-layouts: 5.49 us -> 0 us
    pallas_call x1 -> x2, Pallas kernels: 101 us -> 78.5 us  [the longest x1 76.9 us: on_device(): pl.pallas_call(kernel, name='head', out_shape=(jax.ShapeDtypeStruct((4, 6...]
    unnamed x3 -> x0, local copies, waits for them, and re-layouts: 2.98 us -> none
where the time goes in v2:
time: 79.5 us; the launch traced here: 79.1 us
  Pallas kernels  78.5 us (99%)
    pallas_call x1, Pallas kernels, on_device(): pl.pallas_call(kernel, name='head', out_shape=(jax.ShapeDtypeStruct((4, 6...  76.9 us

profile of v2, /device:TPU:0, one launch (start us, length us, event | category | flops | bytes accessed | tf_op | source)
XLA Modules:
  0.0 79.1 jit_solution(16433549285626138838)
XLA Ops:
  0.6 76.9 %head.1 = (f32[4,64]{1,0:T(4,128)}, bf16[4,8,1792]{2,1,0:T(8,128)(2,1)}) custom-call(bf16[4,2,7168]{2,1,0:T(2,128)(2,1)} %h_ref.1, f32[1,7168]{1,0:T(1,128)} %bitcast.1, s32[4,64]{1,0:T(4,128)} %t_ref.1, bf16[2560,1792]{1,0:T(8,128)(2,1)} %w_hbm.1, bf16[2560,1792]{1,0:T(8,128)(2,1)} %e_hbm.1), custom_call_target="tpu_custom_call" | custom-call | tf_op jit(solution)/shard_map/head/pallas_call | solution.py:474
  77.6 1.6 %results.1 = (f32[4,64]{1,0:T(4,128)}, bf16[4,8,1792]{2,1,0:T(8,128)(2,1)}) custom-call(f32[4,64]{1,0:T(4,128)} %get-tuple-element.4.logp_ref, bf16[4,8,1792]{2,1,0:T(8,128)(2,1)} %get-tuple-element.5.emb_ref), custom_call_target="tpu_custom_call" | custom-call | tf_op jit(solution)/shard_map/results/pallas_call | solution.py:513

commit v3 on v2

--- a/solution.py
+++ b/solution.py
@@ -233,7 +233,7 @@
             cp.wait_recv()
 
         def block(n, _):
-            of = (y + n + 2) % 4
+            of = (y + ((54 >> (2 * n)) & 3)) % 4
             i = ((zh + of // 2) % 2) * 2 + (c + of % 2) % 2
             token = jnp.broadcast_to(TOK[i][0:1], (QB, 256)).T
             first = vo * VOC
@@ -242,7 +242,8 @@
                 entry = (lax.broadcasted_iota(i32, (256, QB), 1) + (first + k * QB)).astype(f32)
                 hot = jnp.where(token == entry, 1.0, 0.0).astype(bf16).reshape(4, 4, 16, QB)
                 for px in range(4):
-                    OH[n, :, (px - x + 6) % 4, :, pl.ds(pl.multiple_of(k * QB, QB), QB)] = hot[:, px]
+                    slot = (135 >> (2 * ((px - x + 4) % 4))) & 3
+                    OH[n, :, slot, :, pl.ds(pl.multiple_of(k * QB, QB), QB)] = hot[:, px]
                 return 0
 
             lax.fori_loop(0, VOC // QB, tile, 0)
@@ -250,9 +251,8 @@
 
         lax.fori_loop(0, 4, block, 0)
 
-    def pick(n, first, lo, hi):
-        part = pl.ds(0, 1) if first else pl.ds(1, 3)
-        slots = 1 if first else 3
+    def pick(n, at, slots):
+        part = pl.ds(at, slots)
 
         def tile(i, _):
             cols = pl.ds(pl.multiple_of(n * LOW + i * 256, 256), 256)
@@ -264,7 +264,7 @@
                 PK[:, :, part, :, cols] = got.reshape(4, 4, slots, 16, 256)
             return 0
 
-        lax.fori_loop(lo, hi, tile, 0)
+        lax.fori_loop(0, (HIGH if n else LOW) // 256, tile, 0)
 
     LO, HI = pl.ds(0, LOW), pl.ds(LOW, HIGH)
 
@@ -277,13 +277,13 @@
         return remote(src, (RA0 if n == 0 else RA1).at[j], a_s.at[n, j], a_r.at[n, j], along(n, ring[j]))
 
     def b_copy(n, j):
-        slot = 3 - 2 * j
+        slot = 1 + j
         src = PK.at[slot, :, :, :, LO] if n == 0 else PK.at[:, :, slot, :, HI]
         return remote(src, (RB0 if n == 0 else RB1).at[j], b_s.at[n, j], b_r.at[n, j], along(n, ring[j]))
 
     def c_copy(n, j):
-        slot = (ring[j] + 2) % 4
-        src = PK.at[2, :, slot, :, LO] if n == 0 else PK.at[slot, :, 2, :, HI]
+        slot = (1, 2, 0)[j]
+        src = PK.at[3, :, slot, :, LO] if n == 0 else PK.at[slot, :, 3, :, HI]
         return remote(src, (RC0 if n == 0 else RC1).at[j], c_s.at[n, j], c_r.at[n, j], along(1 - n, ring[j]))
 
     def a_send(n):
@@ -292,7 +292,7 @@
 
     def b_send(n):
         for j in range(2):
-            slot = 3 - 2 * j
+            slot = 1 + j
             a_copy(n, j).wait_recv()
             for s in range(2):
                 if n == 0:
@@ -306,9 +306,9 @@
             b_copy(n, j).wait_recv()
         for s in range(4):
             if n == 0:
-                PK[2, s, :, :, LO] = PK[2, s, :, :, LO] + (RB0[0, s] + RB0[1, s])
+                PK[3, s, :, :, LO] = PK[3, s, :, :, LO] + (RB0[0, s] + RB0[1, s])
             else:
-                PK[:, s, 2, :, HI] = PK[:, s, 2, :, HI] + (RB1[0, :, s] + RB1[1, :, s])
+                PK[:, s, 3, :, HI] = PK[:, s, 3, :, HI] + (RB1[0, :, s] + RB1[1, :, s])
         for j in range(3):
             go(c_copy(n, j))
 
@@ -320,7 +320,7 @@
             for j in range(3):
                 c_copy(n, j).wait_recv()
             got = RC0 if n == 0 else RC1
-            total.append(PK[2, :, 2, :, LO if n == 0 else HI] + (got[0] + got[1] + got[2]))
+            total.append(PK[3, :, 3, :, LO if n == 0 else HI] + (got[0] + got[1] + got[2]))
         total = jnp.concatenate(total, axis=2).astype(f32)
         first, second = total[:, :8, :].reshape(32, WID), total[:, 8:, :].reshape(32, WID)
         mine = zl == 0
@@ -401,53 +401,55 @@
         row = moved[0:1] + moved[1:2] + moved[2:3]
         logp_ref[...] = jnp.concatenate([row[:, 64 * s : 64 * (s + 1)] for s in range(4)], axis=0)
 
-    restore(0)
     first_unit()
     p1_send(0)
+    restore(0)
     restore(1)
-    one_hot()
     p1_wait(0)
     p2_send(0)
-    for cp in e_cps:
-        cp.wait()
-    pick(0, True, 0, 4)
-    a_send(0)
+    one_hot()
     other_units()
     p1_send(1)
     p1_send(2)
     p1_send(3)
-    pick(1, True, 0, 3)
+    for cp in e_cps:
+        cp.wait()
+    pick(0, 0, 1)
+    a_send(0)
+    pick(1, 0, 1)
+    p1_wait(1)
+    p2_send(1)
     a_send(1)
     restore(2)
     restore(3)
-    p1_wait(1)
-    p2_send(1)
+    p1_wait(2)
+    p2_send(2)
+    p1_wait(3)
+    p2_send(3)
     gathered(0)
     chunk(0)
-    p1_wait(2)
-    p1_wait(3)
-    p2_send(2)
-    p2_send(3)
-    pick(0, False, 0, 4)
+    pick(0, 1, 2)
     p3_send(1)
     b_send(0)
-    pick(1, False, 0, 3)
+    pick(1, 1, 2)
     b_send(1)
     p3_send(2)
     p3_send(3)
+    pick(0, 3, 1)
+    pick(1, 3, 1)
     gathered(1)
     chunk(1)
     c_send(0)
-    c_send(1)
     gathered(2)
     chunk(2)
+    c_send(1)
+    early = stats(0)
     gathered(3)
     chunk(3)
-    early = stats(0)
+    first_send(early, stats(1))
     kept = d_send()
-    first_send(early, stats(1))
+    second_send()
     d_done(kept)
-    second_send()
     finish()
     for k in range(4):
         for m in range(HM):

time: 79.5 us -> 75.1 us (0.945)
  Pallas kernels: 78.5 us -> 74.1 us
    pallas_call x1, Pallas kernels: 76.9 us -> 72.6 us  [on_device(): pl.pallas_call(kernel, name='head', out_shape=(jax.ShapeDtypeStruct((4, 6...]
where the time goes in v3:
time: 75.1 us; the launch traced here: 74.8 us
  Pallas kernels  74.1 us (99%)
    pallas_call x1, Pallas kernels, on_device(): pl.pallas_call(kernel, name='head', out_shape=(jax.ShapeDtypeStruct((4, 6...  72.6 us
    pallas_call x1, Pallas kernels, on_device(): pl.pallas_call(hand_over, name='results', out_shape=(jax.ShapeDtypeStruct...  1.56 us

profile of v3, /device:TPU:0, one launch (start us, length us, event | category | flops | bytes accessed | tf_op | source)
XLA Modules:
  0.0 74.8 jit_solution(8575215690480864896)
XLA Ops:
  0.6 72.6 %head.1 = (f32[4,64]{1,0:T(4,128)}, bf16[4,8,1792]{2,1,0:T(8,128)(2,1)}) custom-call(bf16[4,2,7168]{2,1,0:T(2,128)(2,1)} %h_ref.1, f32[1,7168]{1,0:T(1,128)} %bitcast.1, s32[4,64]{1,0:T(4,128)} %t_ref.1, bf16[2560,1792]{1,0:T(8,128)(2,1)} %w_hbm.1, bf16[2560,1792]{1,0:T(8,128)(2,1)} %e_hbm.1), custom_call_target="tpu_custom_call" | custom-call | tf_op jit(solution)/shard_map/head/pallas_call | solution.py:476
  73.2 1.6 %results.1 = (f32[4,64]{1,0:T(4,128)}, bf16[4,8,1792]{2,1,0:T(8,128)(2,1)}) custom-call(f32[4,64]{1,0:T(4,128)} %get-tuple-element.4.logp_ref, bf16[4,8,1792]{2,1,0:T(8,128)(2,1)} %get-tuple-element.5.emb_ref), custom_call_target="tpu_custom_call" | custom-call | tf_op jit(solution)/shard_map/results/pallas_call | solution.py:515

commit v4 on v3

--- a/solution.py
+++ b/solution.py
@@ -29,9 +29,9 @@
 
 
 def kernel(
-    h_ref, g_ref, t_ref, w_hbm, e_hbm, logp_ref, emb_ref,
-    W, EM, OH, US, UR, TOK, PERM, X, PS, PR, ZS, ZR, OWN, PK, RA0, RA1, RB0, RB1, RC0, RC1, RD, SD, SA, SB,
-    w_sem, e_sem, us_s, us_r, tk_s, tk_r, p1_s, p1_r, p2_s, p2_r, p3_s, p3_r,
+    h_hbm, g_hbm, t_hbm, w_hbm, e_hbm, logp_ref, emb_ref,
+    h_ref, g_ref, t_ref, W, EM, OH, US, UR, TOK, PERM, X, PS, PR, ZS, ZR, OWN, PK, RA0, RA1, RB0, RB1, RC0, RC1, RD, SD, SA, SB,
+    in_sem, w_sem, e_sem, us_s, us_r, tk_s, tk_r, p1_s, p1_r, p2_s, p2_r, p3_s, p3_r,
     co_s, co_r, z_s, z_r, a_s, a_r, b_s, b_r, c_s, c_r, d_s, d_r, sa_s, sa_r, sb_s, sb_r,
 ):
     fs, vo = lax.axis_index("fsdp"), lax.axis_index("vocab")
@@ -54,6 +54,21 @@
     def go(cp):
         cp.start()
         sends.append(cp)
+
+    barrier = pltpu.get_barrier_semaphore()
+    peers = [dev(x, y, z + dz, c + dc) for dz, dc in column[1:]]
+    peers += [dev(x + dx, y + dy, z, c) for dx, dy in plane[1:]]
+    for peer in peers:
+        pl.semaphore_signal(barrier, inc=1, device_id=peer, device_id_type=MESH)
+
+    in_cps = [
+        pltpu.make_async_copy(src, dst, in_sem.at[i])
+        for i, (src, dst) in enumerate(((h_hbm, h_ref), (g_hbm, g_ref), (t_hbm, t_ref)))
+    ]
+    for cp in in_cps:
+        cp.start()
+    for cp in in_cps:
+        cp.wait()
 
     w_cps = [
         pltpu.make_async_copy(w_hbm.at[pl.ds(i * 640, 640)], W.at[pl.ds(i * 640, 640)], w_sem.at[i])
@@ -65,12 +80,6 @@
     ]
     for cp in w_cps[:2] + e_cps + w_cps[2:]:
         cp.start()
-
-    barrier = pltpu.get_barrier_semaphore()
-    peers = [dev(x, y, z + dz, c + dc) for dz, dc in column[1:]]
-    peers += [dev(x + dx, y + dy, z, c) for dx, dy in plane[1:]]
-    for peer in peers:
-        pl.semaphore_signal(barrier, inc=1, device_id=peer, device_id_type=MESH)
 
     h = jnp.concatenate([h_ref[s].astype(f32) for s in range(4)], axis=0)
     ms = jnp.sum(h * h, axis=1, keepdims=True) * (1.0 / D)
@@ -477,9 +486,12 @@
         kernel,
         name="head",
         out_shape=(jax.ShapeDtypeStruct((4, 64), f32), jax.ShapeDtypeStruct((4, 8, WID), bf16)),
-        in_specs=[vm, vm, vm, hbm, hbm],
+        in_specs=[hbm] * 5,
         out_specs=(vm, vm),
         scratch_shapes=[
+            pltpu.VMEM((4, 2, D), bf16),
+            pltpu.VMEM((1, D), f32),
+            pltpu.VMEM((4, 64), i32),
             pltpu.VMEM((VOC, WID), bf16),
             pltpu.VMEM((VOC, WID), bf16),
             pltpu.VMEM((4, 4, 4, 16, VOC), bf16),
@@ -504,6 +516,7 @@
             pltpu.VMEM((32, WID), bf16),
             pltpu.VMEM((5, 8, 256), f32),
             pltpu.VMEM((16, 8, 256), f32),
+            dma((3,)),
             dma((4,)),
             dma((2,)),
             *sems,

time: 75.1 us -> 74.4 us (level)
  no operation moved by 1% of the time
where the time goes in v4:
time: 74.4 us; the launch traced here: 74.1 us
  Pallas kernels  73.5 us (99%)
    pallas_call x1, Pallas kernels, on_device(): pl.pallas_call(kernel, name='head', out_shape=(jax.ShapeDtypeStruct((4, 6...  71.9 us
    pallas_call x1, Pallas kernels, on_device(): pl.pallas_call(hand_over, name='results', out_shape=(jax.ShapeDtypeStruct...  1.56 us

profile of v4, /device:TPU:0, one launch (start us, length us, event | category | flops | bytes accessed | tf_op | source)
XLA Modules:
  0.0 74.1 jit_solution(13566421602489622527)
XLA Ops:
  0.6 71.9 %head.1 = (f32[4,64]{1,0:T(4,128)}, bf16[4,8,1792]{2,1,0:T(8,128)(2,1)}) custom-call(bf16[4,2,7168]{2,1,0:T(2,128)(2,1)} %h_hbm.1, f32[1,7168]{1,0:T(1,128)} %bitcast.1, s32[4,64]{1,0:T(4,128)} %t_hbm.1, bf16[2560,1792]{1,0:T(8,128)(2,1)} %w_hbm.1, bf16[2560,1792]{1,0:T(8,128)(2,1)} %e_hbm.1), custom_call_target="tpu_custom_call" | custom-call | tf_op jit(solution)/shard_map/head/pallas_call | solution.py:485
  72.5 1.6 %results.1 = (f32[4,64]{1,0:T(4,128)}, bf16[4,8,1792]{2,1,0:T(8,128)(2,1)}) custom-call(f32[4,64]{1,0:T(4,128)} %get-tuple-element.4.logp_ref, bf16[4,8,1792]{2,1,0:T(8,128)(2,1)} %get-tuple-element.5.emb_ref), custom_call_target="tpu_custom_call" | custom-call | tf_op jit(solution)/shard_map/results/pallas_call | solution.py:528

commit v5 on v4

--- a/solution.py
+++ b/solution.py
@@ -444,10 +444,10 @@
     b_send(1)
     p3_send(2)
     p3_send(3)
+    gathered(1)
+    chunk(1)
     pick(0, 3, 1)
     pick(1, 3, 1)
-    gathered(1)
-    chunk(1)
     c_send(0)
     gathered(2)
     chunk(2)
@@ -470,9 +470,15 @@
         cp.wait_send()
 
 
-def hand_over(logp_ref, emb_ref, logp_out, emb_out):
-    logp_out[...] = logp_ref[...]
-    emb_out[...] = emb_ref[...]
+def hand_over(logp_ref, emb_ref, logp_out, emb_out, sem):
+    cps = [
+        pltpu.make_async_copy(emb_ref, emb_out, sem.at[0]),
+        pltpu.make_async_copy(logp_ref, logp_out, sem.at[1]),
+    ]
+    for cp in cps:
+        cp.start()
+    for cp in cps:
+        cp.wait()
 
 
 def on_device(head_table, embed_table, hidden, norm_gain, tokens):
@@ -529,8 +535,9 @@
         hand_over,
         name="results",
         out_shape=(jax.ShapeDtypeStruct((4, 64), f32), jax.ShapeDtypeStruct((4, 8, WID), bf16)),
-        in_specs=[vm, vm],
-        out_specs=(vm, vm),
+        in_specs=[hbm, hbm],
+        out_specs=(hbm, hbm),
+        scratch_shapes=[dma((2,))],
     )(logp, emb)
 
 

time: 74.4 us -> 77.4 us (1.040)
  Pallas kernels: 73.5 us -> 76.6 us
    pallas_call x1, Pallas kernels: 1.56 us -> 4.66 us  [on_device(): pl.pallas_call(hand_over, name='results', out_shape=(jax.ShapeDtypeStruct...]
where the time goes in v5:
time: 77.4 us; the launch traced here: 77.2 us
  Pallas kernels  76.6 us (99%)
    pallas_call x1, Pallas kernels, on_device(): pl.pallas_call(kernel, name='head', out_shape=(jax.ShapeDtypeStruct((4, 6...  71.9 us
    pallas_call x1, Pallas kernels, on_device(): pl.pallas_call(hand_over, name='results', out_shape=(jax.ShapeDtypeStruct...  4.66 us

profile of v5, /device:TPU:0, one launch (start us, length us, event | category | flops | bytes accessed | tf_op | source)
XLA Modules:
  0.0 77.2 jit_solution(15982452460790366565)
XLA Ops:
  0.6 71.9 %head.1 = (f32[4,64]{1,0:T(4,128)}, bf16[4,8,1792]{2,1,0:T(8,128)(2,1)}) custom-call(bf16[4,2,7168]{2,1,0:T(2,128)(2,1)} %h_hbm.1, f32[1,7168]{1,0:T(1,128)} %bitcast.1, s32[4,64]{1,0:T(4,128)} %t_hbm.1, bf16[2560,1792]{1,0:T(8,128)(2,1)} %w_hbm.1, bf16[2560,1792]{1,0:T(8,128)(2,1)} %e_hbm.1), custom_call_target="tpu_custom_call" | custom-call | tf_op jit(solution)/shard_map/head/pallas_call | solution.py:491
  72.5 4.7 %results.1 = (f32[4,64]{1,0:T(4,128)}, bf16[4,8,1792]{2,1,0:T(8,128)(2,1)}) custom-call(f32[4,64]{1,0:T(4,128)} %get-tuple-element.4.logp_ref, bf16[4,8,1792]{2,1,0:T(8,128)(2,1)} %get-tuple-element.5.emb_ref), custom_call_target="tpu_custom_call" | custom-call | tf_op jit(solution)/shard_map/results/pallas_call | solution.py:534
